TPU v7x, 256 devices: a whole 4x4x8 slice. The times are simulated.
256 devices in a mesh: vocab: 64 (over y, z_hi, x), tok: 4 (over z_lo, core).
Axes of the slice: x: 4, y: 4, z: 8 (z_hi: 4, z_lo: 2; z = z_hi * 2 + z_lo), core: 2. Of those that a mesh axis runs over, the one named last changes fastest.
Arguments:
- hidden: bfloat16 [768, 3072], P('tok', 'vocab'), may hold values from -40 to 40
- hidden_tangent: bfloat16 [768, 3072], P('tok', 'vocab'), may hold values from -6 to 6
- head: bfloat16 [3072, 65536], P('tok', 'vocab'), may hold values from -2 to 2
- head_tangent: bfloat16 [3072, 65536], P('tok', 'vocab'), may hold values from -0.109375 to 0.109375
- ref_logits: bfloat16 [768, 65536], P('tok', 'vocab'), may hold values from -240 to 240
- actions: int32 [768], P('tok'), may hold values from 0 to 65535
- valid: int32 [768], P('tok'), may hold values 0 or 1
Outputs:
- head_product: bfloat16 [3072, 65536], P('tok', 'vocab')
- hidden_product: bfloat16 [768, 3072], P('tok', 'vocab')
- penalty: float32 [768], P('tok')
- action_logprob: float32 [768], P('tok')
All inputs are finite; a program needn't handle non-finite values. No bound on the sum of `valid` on one device may be relied on, other than what follows from the above.
Results may differ from a plain program's by a relative error of at most 0.008.
Values may be sent and summed in bfloat16 or wider, within the bound.
A program may use at most 64 MiB of HBM per device.

v0:
```python
import jax
import jax.numpy as jnp
from jax import lax
from jax.sharding import PartitionSpec as P


def body(hidden, hidden_tangent, head, head_tangent, ref_logits, actions, valid):
    full_hidden, full_tangent = (
        lax.all_gather(hidden, "vocab", axis=1, tiled=True),
        lax.all_gather(hidden_tangent, "vocab", axis=1, tiled=True),
    )
    vocab_cols = head.shape[1]
    full_head, full_head_tangent = (
        lax.all_gather(head, "tok", axis=0, tiled=True),
        lax.all_gather(head_tangent, "tok", axis=0, tiled=True),
    )
    logits = jnp.dot(full_hidden, full_head, preferred_element_type=jnp.float32)
    tangent = jnp.dot(full_hidden, full_head_tangent, preferred_element_type=jnp.float32) + jnp.dot(
        full_tangent, full_head, preferred_element_type=jnp.float32
    )
    local_index = actions - lax.axis_index("vocab") * vocab_cols
    picked = lax.broadcasted_iota(jnp.int32, logits.shape, 1) == local_index[:, None]
    chosen = jnp.sum(jnp.where(picked, logits, 0.0), 1)
    ref_float = ref_logits.astype(jnp.float32)
    local_top = jnp.max(logits, 1)
    local_ref_top = jnp.max(ref_float, 1)
    top, ref_top = lax.pmax((local_top, local_ref_top), "vocab")
    weights = jnp.exp(logits - top[:, None])
    ref_weights = jnp.exp(ref_float - ref_top[:, None])
    total, moment, ref_sum, cross, action_logit = lax.psum(
        (
            jnp.sum(weights, 1),
            jnp.sum(weights * tangent, 1),
            jnp.sum(ref_weights, 1),
            jnp.sum(ref_weights * (ref_float - logits), 1),
            chosen,
        ),
        "vocab",
    )
    log_total = top + jnp.log(total)
    mean_tangent = moment / total
    valid_float = valid.astype(jnp.float32)
    penalty = valid_float * (cross / ref_sum - (ref_top + jnp.log(ref_sum)) + log_total)
    action_logprob = action_logit - log_total
    probs = jnp.exp(logits - log_total[:, None])
    fisher = (valid_float[:, None] * probs * (tangent - mean_tangent[:, None])).astype(jnp.bfloat16)
    head_product = lax.psum_scatter(
        lax.dot_general(
            full_hidden, fisher, (((0,), (0,)), ((), ())), preferred_element_type=jnp.float32
        ),
        "tok",
        scatter_dimension=0,
        tiled=True,
    ).astype(jnp.bfloat16)
    hidden_part = lax.psum_scatter(
        lax.dot_general(
            full_head, fisher, (((1,), (1,)), ((), ())), preferred_element_type=jnp.float32
        ),
        "vocab",
        scatter_dimension=0,
        tiled=True,
    )
    hidden_product = hidden_part.T.astype(jnp.bfloat16)
    return (head_product, hidden_product, penalty, action_logprob)


def solution(mesh):
    return jax.shard_map(
        body,
        mesh=mesh,
        in_specs=(
            P("tok", "vocab"),
            P("tok", "vocab"),
            P("tok", "vocab"),
            P("tok", "vocab"),
            P("tok", "vocab"),
            P("tok"),
            P("tok"),
        ),
        out_specs=(P("tok", "vocab"), P("tok", "vocab"), P("tok"), P("tok")),
        check_vma=False,
    )
```

profile of v0, /device:TPU:34, one launch (start us, length us, event | category | flops | bytes accessed | tf_op | source)
XLA Modules:
  0.0 936.2 jit_solution(4687779721472320464)
XLA Ops:
  7.2 0.7 all-gather.5.cloned.1.call-update
  8.0 0.7 all-gather.7.cloned.1.call-update
  8.7 0.7 all-gather.9.cloned.1.call-update
  10.7 0.6 broadcast_subtract_fusion
  11.3 77.7 %all-gather.5.cloned.1.call-done = bf16[192,3072]{0,1:T(8,128)(2,1)} async-done(((bf16[192,48]{0,1:T(8,128)(2,1)}), bf16[192,3072]{0,1:T(8,128)(2,1)}) %all-gather.5.cloned.1.call-update) | async-done | bytes 1179664 | tf_op jit(solution)/shard_map/all_gather | solution.py:9
  89.0 65.7 %all-gather.7.cloned.1.call-done = bf16[3072,1024]{1,0:T(8,128)(2,1)} async-done(((bf16[768,1024]{1,0:T(8,128)(2,1)}), bf16[3072,1024]{1,0:T(8,128)(2,1)}) %all-gather.7.cloned.1.call-update) | async-done | bytes 6291472 | tf_op jit(solution)/shard_map/all_gather | solution.py:14
  154.7 4.8 fusion.6
  159.5 189.5 %all-reduce.1 = (f32[192]{0:T(256)}, f32[192]{0:T(256)S(1)}) all-reduce(bf16[192]{0:T(256)(128)(2,1)S(1)} %reduce_max.24, f32[192]{0:T(256)S(1)} %get-tuple-element.29), channel_id=1, replica_groups=mesh['vocab'=64,'tok'=4] {'vocab'}, use_global_device_ids=true, to_apply=%region_9.10 | all-reduce | flops 384 | bytes 2688 | tf_op jit(solution)/shard_map/pmax | solution.py:27
  349.0 5.1 fusion.7
  354.1 5.8 select_reduce_fusion
  359.9 195.3 %all-reduce = (f32[192]{0:T(256)S(1)}, f32[192]{0:T(256)S(1)}, f32[192]{0:T(256)}, f32[192]{0:T(256)}, f32[192]{0:T(256)S(1)}) all-reduce(f32[192]{0:T(256)S(1)} %get-tuple-element.16, f32[192]{0:T(256)} %get-tuple-element.17, f32[192]{0:T(256)} %get-tuple-element.18, ...), channel_id=1, replica_groups=mesh['vocab'=64,'tok'=4] {'vocab'}, use_global_device_ids=true, to_apply=%region_5.6 | all-reduce | flops 960 | bytes 7680 | tf_op jit(solution)/shard_map/psum | solution.py:30
  555.2 0.6 fusion.5
  555.8 0.9 multiply_convert_fusion
  556.6 6.4 convolution_bitcast_fusion.1
  563.1 3.4 copy.15
  566.5 6.5 convolution_bitcast_fusion
  573.0 0.6 copy-done.2
  573.7 0.6 add_multiply_fusion
  574.3 235.8 %reduce-scatter.7.cloned.1.call-done = f32[48,192]{1,0:T(8,128)} async-done(((f32[3072,192]{1,0:T(8,128)}), f32[48,192]{1,0:T(8,128)}) %reduce-scatter.7.cloned.1.call-update) | async-done | bytes 36880
  810.2 0.9 copy.16
  811.1 0.7 copy.14
  811.8 113.9 %reduce-scatter.5.cloned.1.call-done = f32[768,1024]{0,1:T(8,128)} async-done(((f32[3072,1024]{0,1:T(8,128)}), f32[768,1024]{0,1:T(8,128)}) %reduce-scatter.5.cloned.1.call-update) | async-done | bytes 3145744 | tf_op jit(solution)/shard_map/reduce_scatter | solution.py:47
  925.7 2.0 convert_element_type.20
  927.8 1.6 copy.13
  (28 shorter events, 1.5 us)
Async XLA Ops:
  7.2 2.9 copy-start.3
  7.2 3.4 copy-start.1
  7.2 3.5 copy-start.5
  7.2 81.8 %all-gather.5.cloned.1.call-start = ((), (), s32[]{:S(2)}) async-start(), calls=%async_computation.2 | async-start | bytes 1597440 | tf_op jit(solution)/shard_map/all_gather | solution.py:9
  7.9 146.8 %all-gather.7.cloned.1.call-start = ((), (), s32[]{:S(2)}) async-start(), calls=%async_computation.3 | async-start | bytes 7864320 | tf_op jit(solution)/shard_map/all_gather | solution.py:14
  8.7 340.3 %all-gather.9.cloned.1.call-start = ((), (), s32[]{:S(2)}) async-start(), calls=%async_computation.4 | async-start | bytes 7864320 | tf_op jit(solution)/shard_map/all_gather | solution.py:15
  9.4 344.7 %all-gather.11.cloned.1.call-start = ((), (), s32[]{:S(2)}) async-start(), calls=%async_computation.5 | async-start | bytes 1597440 | tf_op jit(solution)/shard_map/all_gather | solution.py:10
  10.0 800.2 %reduce-scatter.7.cloned.1.call-start = ((), (), s32[]{:S(2)}) async-start(), calls=%async_computation.7 | async-start | bytes 3194880
  89.0 260.0 %copy-start = (bf16[192,3072]{0,1:T(8,128)(2,1)S(1)}, bf16[192,3072]{0,1:T(8,128)(2,1)}, u32[]{:S(2)}) copy-start(bf16[192,3072]{0,1:T(8,128)(2,1)} %all-gather.5.cloned.1.call-done) | copy-start | bytes 3538948
  566.5 359.2 %reduce-scatter.5.cloned.1.call-start = ((), (), s32[]{:S(2)}) async-start(), calls=%async_computation.6 | async-start | bytes 15728640 | tf_op jit(solution)/shard_map/reduce_scatter | solution.py:47
  573.0 0.7 copy-start.2
  573.0 0.7 copy-start.4
  573.0 0.7 copy-start.6
  573.0 0.7 copy-start.7
Sparse Core Ops, SparseCore 0:
  11.3 77.6 all-gather.4
  90.8 63.8 all-gather.6
  156.6 66.8 all-gather.8
  226.6 78.9 all-gather.10
  566.6 243.4 reduce-scatter.6
  812.6 113.0 reduce-scatter.4
where the time goes:
time: 939 us; the launch traced here: 936 us
  waiting for transfers between devices  496 us (53%)
  blocking collectives  385 us (41%)
  matrix products  28.6 us (3%)
  between operations  14.2 us (2%)
    unnamed x7, waiting for transfers between devices  238 us
    psum x1, blocking collectives, body(): lax.psum((jnp.sum(weights, 1), jnp.sum(weights * tangent, 1), jnp.sum(ref...  195 us
    pmax x1, blocking collectives, body(): top, ref_top = lax.pmax((local_top, local_ref_top), 'vocab')  189 us
    reduce_scatter x1, waiting for transfers between devices, body(): lax.psum_scatter(lax.dot_general(full_hidden, fisher, (((0,), (0,)), ((),...  114 us
    all_gather x1, waiting for transfers between devices, body(): lax.all_gather(hidden, 'vocab', axis=1, tiled=True)  77.7 us
    all_gather x1, waiting for transfers between devices, body(): lax.all_gather(head, 'tok', axis=0, tiled=True)  65.7 us
  transfers between devices with their start and end apart: 6, of which 4 were waited for; matrix products, arithmetic and copies ran while one was open for 2% of the time, Pallas kernels for 0%

commit v1 on v0

v1 whole, which is shorter than its diff:
```python
import functools

import jax
import jax.numpy as jnp
from jax import lax
from jax.experimental import pallas as pl
from jax.experimental.pallas import tpu as pltpu
from jax.sharding import PartitionSpec as P

F32 = jnp.float32
BF16 = jnp.bfloat16
MESH = pl.DeviceIdType.MESH
ORDER = (3, 2, 1, 0)


def low_lanes(rows):
    return lax.broadcasted_iota(jnp.int32, (rows, 128), 1) < 64


def swap_halves(value):
    return pltpu.roll(value, 64, 1)


def merge(stats):
    tops = [s[0:1] for s in stats]
    ref_tops = [s[3:4] for s in stats]
    top = functools.reduce(jnp.maximum, tops)
    ref_top = functools.reduce(jnp.maximum, ref_tops)
    scale = [jnp.exp(a - top) for a in tops]
    ref_scale = [jnp.exp(a - ref_top) for a in ref_tops]
    n = range(len(stats))
    return (
        top,
        sum(stats[i][1:2] * scale[i] for i in n),
        sum(stats[i][2:3] * scale[i] for i in n),
        ref_top,
        sum(stats[i][4:5] * ref_scale[i] for i in n),
        sum(stats[i][5:6] * ref_scale[i] for i in n),
        sum(stats[i][6:7] for i in n),
    )


def kernel(
    s_ref, head_ref, ht_ref, ref_ref, act_ref, val_ref,
    hp_ref, hid_ref, tok_ref,
    head_t, ht_t, ref_t, ybuf, hbuf, hun, tun,
    out3, in3, out1, in1, xl, xt, rl, rt, lg, tg,
    sst, sbuf, fbuf, fun, ep,
    e1s, e1r, e2s, e2r, zsend, zrecv, ysend, yrecv,
    ya_s, ya_r, za_s, za_r, xa_s, xa_r, b3_s, b3_r, b1_s, b1_r, bl_s, bl_r, bt_s, bt_r,
    c_s, c_r, d1_s, d1_r, d2_s, d2_r, d3_s, d3_r, e1_s, e1_q, e2_s, e2_q, ez_s, ez_r, ey_s, ey_r,
):
    v = lax.axis_index("vocab")
    t = lax.axis_index("tok")
    y, zh, x = v // 16, (v // 4) % 4, v % 4
    zl, c = t // 2, t % 2

    def at_x(d):
        return (v - x + (x + d) % 4, t)

    def at_y(d):
        return ((y + d) % 4 * 16 + zh * 4 + x, t)

    def tok_of(r):
        return (zl + r // 2) % 2 * 2 + (c + r % 2) % 2

    def at_z(r, d):
        return (y * 16 + (zh + d) % 4 * 4 + x, tok_of(r))

    def send(src, dst, ssem, rsem, device):
        return pltpu.make_async_remote_copy(
            src_ref=src, dst_ref=dst, send_sem=ssem, recv_sem=rsem,
            device_id=device, device_id_type=MESH,
        )

    barrier = pltpu.get_barrier_semaphore()
    column = [(r, d) for r in ORDER for d in range(4) if (r, d) != (0, 0)]
    peers = [at_x(d) for d in (1, 2, 3)] + [at_y(d) for d in (1, 2, 3)] + [at_z(r, d) for r, d in column]
    for peer in peers:
        pl.semaphore_signal(barrier, inc=1, device_id=peer, device_id_type=MESH)
    pl.semaphore_wait(barrier, len(peers))

    y_copies = [send(s_ref, ybuf.at[y], ya_s.at[d], ya_r.at[d], at_y(d + 1)) for d in range(3)]
    for copy in y_copies:
        copy.start()
    ybuf[y] = s_ref[...]
    for copy in y_copies:
        copy.wait_recv()

    z_copies = {
        (r, d): send(ybuf.at[tok_of(r)], hbuf.at[r, zh, x], za_s.at[r * 4 + d], za_r.at[r * 4 + d], at_z(r, d))
        for r, d in column
    }
    for key in column:
        z_copies[key].start()
    hbuf[0, zh, x] = ybuf[t]

    for j in range(4):
        for half in range(2):
            cols = slice(half * 512 + j * 128, half * 512 + j * 128 + 128)
            head_t[j, half * 128 : half * 128 + 128] = head_ref[:, cols].T
            ht_t[j, half * 128 : half * 128 + 128] = ht_ref[:, cols].T
            ref_t[j, half * 128 : half * 128 + 128] = ref_ref[0:128, cols].astype(F32).T
        a, b = slice(j * 128, j * 128 + 128), slice(512 + j * 128, 512 + j * 128 + 128)
        tails = jnp.concatenate([ref_ref[128:192, a].astype(F32), ref_ref[128:192, b].astype(F32)], axis=0)
        ref_t[j, 256:384] = tails.T

    left_x, right_x = (x + 3) % 4, (x + 1) % 4
    x_first, x_second = {}, {}
    for r in ORDER:
        own = hbuf.at[r, :, x]
        x_first[r] = (
            send(own, own, xa_s.at[r, 0], xa_r.at[r, 0], at_x(1)),
            send(own, own, xa_s.at[r, 1], xa_r.at[r, 1], at_x(3)),
        )
        from_left = hbuf.at[r, 0:2, left_x]
        from_right = hbuf.at[r, 2:4, right_x]
        x_second[r] = (
            send(from_left, from_left, xa_s.at[r, 2], xa_r.at[r, 2], at_x(1)),
            send(from_right, from_right, xa_s.at[r, 3], xa_r.at[r, 3], at_x(3)),
        )

    def x_start(r):
        for d in range(4):
            if (r, d) != (0, 0):
                z_copies[r, d].wait_recv()
        for copy in x_first[r]:
            copy.start()

    def x_forward(r):
        for first, second in zip(x_first[r], x_second[r]):
            first.wait_recv()
            second.start()

    def unpack(r):
        for copy in x_second[r]:
            copy.wait_recv()
        low = low_lanes(768)
        block = hbuf[r].reshape(768, 384)
        tails = block[:, 256:384].astype(F32)
        other = swap_halves(tails)
        hun[:, r * 256 : r * 256 + 128] = block[:, 0:128]
        hun[:, r * 256 + 128 : r * 256 + 256] = jnp.where(low, tails, other).astype(BF16)
        tun[:, 0:128] = block[:, 128:256]
        tun[:, 128:256] = jnp.where(low, other, tails).astype(BF16)

    low128 = low_lanes(128)

    def pack(value):
        tail = jnp.where(low128, value[0:128, 128:256], value[128:256, 128:256])
        return value[:, 0:128], tail

    def partial(r, j):
        h = hun[:, r * 256 : r * 256 + 256]
        logits = jnp.dot(head_t[j], h, preferred_element_type=F32)
        tangent = jnp.dot(head_t[j], tun[...], preferred_element_type=F32) + jnp.dot(
            ht_t[j], h, preferred_element_type=F32
        )
        return pack(logits) + pack(tangent)

    sibling = (v, tok_of(1))
    across = (v, tok_of(2))

    def to_sibling(j, out, into, ssem, rsem):
        return send(out.at[j], into.at[j], ssem.at[j], rsem.at[j], sibling)

    def cross_l(j):
        return send(xl.at[j], rl.at[j], bl_s.at[j], bl_r.at[j], across)

    def cross_t(j):
        return send(xt.at[j], rt.at[j], bt_s.at[j], bt_r.at[j], across)

    def give(r, out, into, ssem, rsem):
        @pl.loop(0, 4)
        def _(j):
            lm, lt, tm, tt = partial(r, j)
            out[j, 0, 0:256] = lm
            out[j, 0, 256:384] = lt
            out[j, 1, 0:256] = tm
            out[j, 1, 256:384] = tt
            to_sibling(j, out, into, ssem, rsem).start()

    x_start(3)
    x_start(2)
    x_forward(3)
    x_start(1)
    x_forward(2)
    x_start(0)
    unpack(3)
    give(3, out3, in3, b3_s, b3_r)
    x_forward(1)
    unpack(2)

    @pl.loop(0, 4)
    def _(j):
        lm, lt, tm, tt = partial(2, j)
        to_sibling(j, out3, in3, b3_s, b3_r).wait_recv()
        xl[j, 0:256] = lm + in3[j, 0, 0:256]
        xl[j, 256:384] = lt + in3[j, 0, 256:384]
        xt[j, 0:256] = (tm + in3[j, 1, 0:256]).astype(BF16)
        xt[j, 256:384] = (tt + in3[j, 1, 256:384]).astype(BF16)
        cross_l(j).start()
        cross_t(j).start()

    x_forward(0)
    unpack(1)
    give(1, out1, in1, b1_s, b1_r)
    unpack(0)

    @pl.loop(0, 4)
    def _(j):
        lm, lt, tm, tt = partial(0, j)
        to_sibling(j, out1, in1, b1_s, b1_r).wait_recv()
        lg[j, 0:256] = lm + in1[j, 0, 0:256]
        lg[j, 256:384] = lt + in1[j, 0, 256:384]
        tg[j, 0:256] = tm + in1[j, 1, 0:256]
        tg[j, 256:384] = tt + in1[j, 1, 256:384]

    lowest = jnp.full((1, 128), -jnp.inf, F32)

    def maxima(j, carry):
        top_m, top_t, ref_m, ref_tl = carry
        cross_l(j).wait_recv()
        cross_t(j).wait_recv()
        logits = lg[j] + rl[j]
        lg[j] = logits
        tg[j] = tg[j] + rt[j].astype(F32)
        ref = ref_t[j]
        return (
            jnp.maximum(top_m, jnp.max(logits[0:256], 0, keepdims=True)),
            jnp.maximum(top_t, jnp.max(logits[256:384], 0, keepdims=True)),
            jnp.maximum(ref_m, jnp.max(ref[0:256], 0, keepdims=True)),
            jnp.maximum(ref_tl, jnp.max(ref[256:384], 0, keepdims=True)),
        )

    top_m, top_t, ref_m, ref_tl = lax.fori_loop(0, 4, maxima, (lowest,) * 4)
    top_t = jnp.maximum(top_t, swap_halves(top_t))
    ref_tl = jnp.maximum(ref_tl, swap_halves(ref_tl))

    row = lax.broadcasted_iota(jnp.int32, (256, 128), 0)
    main_col = jnp.where(row < 128, row, row + 384)
    tail_row = lax.broadcasted_iota(jnp.int32, (128, 128), 0)
    tail_col = jnp.where(low128, tail_row, tail_row + 512)
    wanted_m = act_ref[:, 0:128] - v * 1024
    wanted_t = act_ref[:, 128:256] - v * 1024

    def sums(j, carry):
        def part(logits, tangent, ref, top, ref_top, col, wanted, old):
            weights = jnp.exp(logits - top)
            ref_weights = jnp.exp(ref - ref_top)
            picked = jnp.where(col + j * 128 == wanted, logits, 0.0)
            new = (weights, weights * tangent, ref_weights, ref_weights * (ref - logits), picked)
            return tuple(o + jnp.sum(n, 0, keepdims=True) for o, n in zip(old, new))

        main = part(lg[j, 0:256], tg[j, 0:256], ref_t[j, 0:256], top_m, ref_m, main_col, wanted_m, carry[0:5])
        tail = part(
            lg[j, 256:384], tg[j, 256:384], ref_t[j, 256:384], top_t, ref_tl, tail_col, wanted_t, carry[5:10]
        )
        return main + tail

    found = lax.fori_loop(0, 4, sums, (jnp.zeros((1, 128), F32),) * 10)
    tails = [value + swap_halves(value) for value in found[5:10]]
    rows_m = [top_m, found[0], found[1], ref_m, found[2], found[3], found[4]]
    rows_t = [top_t, tails[0], tails[1], ref_tl, tails[2], tails[3], tails[4]]
    for i in range(7):
        sst[0, i : i + 1, 0:128] = rows_m[i]
        sst[0, i : i + 1, 128:256] = rows_t[i]
    sst[:, 7:8] = jnp.zeros((3, 1, 256), F32)

    c_copies = []
    for k, place in enumerate((at_x, at_y, lambda d: at_z(0, d))):
        now = [send(sst.at[k], sbuf.at[k, d], c_s.at[k, d], c_r.at[k, d], place(d + 1)) for d in range(3)]
        for copy in now:
            copy.start()
        for copy in now:
            copy.wait_recv()
        merged = merge([sst[k], sbuf[k, 0], sbuf[k, 1], sbuf[k, 2]])
        if k < 2:
            for i in range(7):
                sst[k + 1, i : i + 1] = merged[i]
        c_copies += now

    top, total, moment, ref_top, ref_sum, cross, chosen = merged
    log_total = top + jnp.log(total)
    mean_tangent = moment / total
    valid = val_ref[...].astype(F32)
    tok_ref[0:1] = valid * (cross / ref_sum - (ref_top + jnp.log(ref_sum)) + log_total)
    tok_ref[1:2] = chosen - log_total

    def d_sibling(j):
        return send(fbuf.at[0, j], fbuf.at[1, j], d1_s.at[j], d1_r.at[j], sibling)

    def d_across(j):
        return send(fbuf.at[0, j], fbuf.at[2, j], d2_s.at[j], d2_r.at[j], across)

    def d_relay(j):
        return send(fbuf.at[2, j], fbuf.at[3, j], d3_s.at[j], d3_r.at[j], sibling)

    @pl.loop(0, 4)
    def _(j):
        def part(rows, lanes):
            return (
                valid[:, lanes] * jnp.exp(lg[j, rows] - log_total[:, lanes]) * (tg[j, rows] - mean_tangent[:, lanes])
            ).astype(BF16)

        fbuf[0, j, 0:256] = part(slice(0, 256), slice(0, 128))
        fbuf[0, j, 256:384] = part(slice(256, 384), slice(128, 256))
        d_across(j).start()
        d_sibling(j).start()

    def unpack_fisher(r):
        for j in range(4):
            block = fbuf[r, j]
            tail = block[256:384]
            zero = jnp.zeros_like(tail)
            for half in range(2):
                rows = slice(half * 512 + j * 128, half * 512 + j * 128 + 128)
                fun[rows, r * 256 : r * 256 + 128] = block[half * 128 : half * 128 + 128]
                fun[rows, r * 256 + 128 : r * 256 + 256] = (
                    jnp.where(low128, tail, zero) if half == 0 else jnp.where(low128, zero, tail)
                )

    low192 = low_lanes(192)

    def hidden_part(p):
        @pl.loop(0, 4)
        def _(k):
            rows = pl.ds(pl.multiple_of(k * 192, 192), 192)
            part = jnp.dot(head_ref[rows, :], fun[:, p * 512 : p * 512 + 512], preferred_element_type=F32)
            even, odd = part[:, 128:256], part[:, 384:512]
            tail = jnp.where(low192, even + swap_halves(even), odd + swap_halves(odd))
            ep[p, k, :, :, 0:128] = part[:, 0:128].reshape(4, 48, 128)
            ep[p, k, :, :, 128:256] = part[:, 256:384].reshape(4, 48, 128)
            ep[p, k, :, :, 256:384] = tail.reshape(4, 48, 128)

    e1, e2 = {}, {}
    for p in range(2):
        for side, d in ((0, 1), (1, 3)):
            e1[p, side] = send(e1s.at[p, side], e1r.at[p, side], e1_s.at[p, side], e1_q.at[p, side], at_x(d))
            e2[p, side] = send(e2s.at[p, side], e2r.at[p, side], e2_s.at[p, side], e2_q.at[p, side], at_x(d))

    def e_first(p):
        far = (x + 2) % 4
        e1s[p, 0] = ep[p, 0:2, far].astype(BF16)
        e1s[p, 1] = ep[p, 2:4, far].astype(BF16)
        e1[p, 0].start()
        e1[p, 1].start()

    def e_second(p):
        e2s[p, 0, 2:4] = ep[p, 2:4, right_x].astype(BF16)
        e2s[p, 1, 0:2] = ep[p, 0:2, left_x].astype(BF16)
        e1[p, 0].wait_recv()
        e2s[p, 0, 0:2] = (ep[p, 0:2, right_x] + e1r[p, 0].astype(F32)).astype(BF16)
        e2[p, 0].start()
        e1[p, 1].wait_recv()
        e2s[p, 1, 2:4] = (ep[p, 2:4, left_x] + e1r[p, 1].astype(F32)).astype(BF16)
        e2[p, 1].start()

    ez = {
        (r, d): send(
            zsend.at[r, (zh + d) % 4], zrecv.at[r, d], ez_s.at[r * 4 + d], ez_r.at[r * 4 + d], at_z(r, d)
        )
        for r, d in column
    }

    def e_third(p):
        e2[p, 0].wait_recv()
        e2[p, 1].wait_recv()
        total_x = (ep[p, :, x] + e2r[p, 0].astype(F32) + e2r[p, 1].astype(F32)).astype(BF16)
        for odd in range(2):
            zsend[p * 2 + odd, :, :, 0:128] = total_x[:, :, odd * 128 : odd * 128 + 128]
            zsend[p * 2 + odd, :, :, 128:256] = total_x[:, :, 256:384]
        for r in (p * 2 + 1, p * 2):
            for d in range(4):
                if (r, d) != (0, 0):
                    ez[r, d].start()

    unpack_fisher(0)
    for j in range(4):
        d_sibling(j).wait_recv()
    unpack_fisher(1)
    for j in range(2):
        d_across(j).wait_recv()
        d_relay(j).start()
    hidden_part(0)
    e_first(0)
    for j in range(2, 4):
        d_across(j).wait_recv()
        d_relay(j).start()
    unpack_fisher(2)
    for j in range(4):
        d_relay(j).wait_recv()
    unpack_fisher(3)
    hidden_part(1)
    e_first(1)
    e_second(0)
    e_second(1)

    @pl.loop(0, 3)
    def _(k):
        rows = pl.ds(pl.multiple_of(k * 256, 256), 256)
        hp_ref[rows, :] = lax.dot_general(
            hun[rows, :], fun[...], (((1,), (1,)), ((), ())), preferred_element_type=F32
        ).astype(BF16)

    e_third(0)
    e_third(1)
    for r in ORDER:
        parts = []
        for d in range(4):
            if (r, d) != (0, 0):
                ez[r, d].wait_recv()
                parts.append(zrecv[r, d].astype(F32))
            else:
                parts.append(zsend[0, zh].astype(F32))
        whole = sum(parts)
        slot = tok_of(r)
        ysend[slot, :, 0:128] = whole[:, 0:128]
        tail = whole[:, 128:256]
        ysend[slot, :, 128:256] = swap_halves(tail) if r % 2 else tail
    ey = [
        send(ysend.at[(y + d + 1) % 4], yrecv.at[d], ey_s.at[d], ey_r.at[d], at_y(d + 1)) for d in range(3)
    ]
    for copy in ey:
        copy.start()
    for copy in ey:
        copy.wait_recv()
    hid_ref[...] = (ysend[y] + yrecv[0] + yrecv[1] + yrecv[2]).astype(BF16)

    for copy in y_copies + list(z_copies.values()) + c_copies + list(ez.values()) + ey:
        copy.wait_send()
    for copies in list(x_first.values()) + list(x_second.values()):
        for copy in copies:
            copy.wait_send()
    for copy in list(e1.values()) + list(e2.values()):
        copy.wait_send()

    @pl.loop(0, 4)
    def _(j):
        to_sibling(j, out3, in3, b3_s, b3_r).wait_send()
        to_sibling(j, out1, in1, b1_s, b1_r).wait_send()
        cross_l(j).wait_send()
        cross_t(j).wait_send()
        d_sibling(j).wait_send()
        d_across(j).wait_send()
        d_relay(j).wait_send()


def body(hidden, hidden_tangent, head, head_tangent, ref_logits, actions, valid):
    h, g = hidden.T, hidden_tangent.T
    stacked = jnp.concatenate([h[:, 0:128], g[:, 0:128], h[:, 128:192], g[:, 128:192]], axis=1)
    acts = jnp.concatenate([actions, actions[128:]])[None, :]
    flags = jnp.concatenate([valid, valid[128:]])[None, :]
    vm, dma = pltpu.VMEM, pltpu.SemaphoreType.DMA
    vmem = pl.BlockSpec(memory_space=pltpu.VMEM)
    head_product, hid, tok = pl.pallas_call(
        kernel,
        out_shape=(
            jax.ShapeDtypeStruct((768, 1024), BF16),
            jax.ShapeDtypeStruct((48, 256), BF16),
            jax.ShapeDtypeStruct((2, 256), F32),
        ),
        in_specs=[vmem] * 6,
        out_specs=(vmem,) * 3,
        scratch_shapes=[
            vm((4, 256, 768), BF16),
            vm((4, 256, 768), BF16),
            vm((4, 384, 128), F32),
            vm((4, 48, 384), BF16),
            vm((4, 4, 4, 48, 384), BF16),
            vm((768, 1024), BF16),
            vm((768, 256), BF16),
            vm((4, 2, 384, 128), F32),
            vm((4, 2, 384, 128), F32),
            vm((4, 2, 384, 128), F32),
            vm((4, 2, 384, 128), F32),
            vm((4, 384, 128), F32),
            vm((4, 384, 128), BF16),
            vm((4, 384, 128), F32),
            vm((4, 384, 128), BF16),
            vm((4, 384, 128), F32),
            vm((4, 384, 128), F32),
            vm((3, 8, 256), F32),
            vm((3, 3, 8, 256), F32),
            vm((4, 4, 384, 128), BF16),
            vm((1024, 1024), BF16),
            vm((2, 4, 4, 48, 384), F32),
            vm((2, 2, 2, 48, 384), BF16),
            vm((2, 2, 2, 48, 384), BF16),
            vm((2, 2, 4, 48, 384), BF16),
            vm((2, 2, 4, 48, 384), BF16),
            vm((4, 4, 48, 256), BF16),
            vm((4, 4, 48, 256), BF16),
            vm((4, 48, 256), F32),
            vm((3, 48, 256), F32),
            dma((3,)), dma((3,)),
            dma((16,)), dma((16,)),
            dma((4, 4)), dma((4, 4)),
            dma((4,)), dma((4,)), dma((4,)), dma((4,)),
            dma((4,)), dma((4,)), dma((4,)), dma((4,)),
            dma((3, 3)), dma((3, 3)),
            dma((4,)), dma((4,)), dma((4,)), dma((4,)), dma((4,)), dma((4,)),
            dma((2, 2)), dma((2, 2)), dma((2, 2)), dma((2, 2)),
            dma((16,)), dma((16,)),
            dma((3,)), dma((3,)),
        ],
        compiler_params=pltpu.CompilerParams(
            collective_id=0, has_side_effects=True, vmem_limit_bytes=56 * 1024 * 1024
        ),
    )(stacked, head, head_tangent, ref_logits, acts, flags)
    return (head_product, hid[:, 0:192].T, tok[0, 0:192], tok[1, 0:192])


def solution(mesh):
    return jax.shard_map(
        body,
        mesh=mesh,
        in_specs=(P("tok", "vocab"),) * 5 + (P("tok"), P("tok")),
        out_specs=(P("tok", "vocab"), P("tok", "vocab"), P("tok"), P("tok")),
        check_vma=False,
    )
```

time: 939 us -> 128 us (0.14)
  waiting for transfers between devices: 496 us -> 0 us
  blocking collectives: 385 us -> 0 us
  Pallas kernels: 0 us -> 112 us
  matrix products: 28.6 us -> 0 us
  between operations: 14.2 us -> 0.64 us
    unnamed x7 -> x0, waiting for transfers between devices: 238 us -> none
    psum x1 -> x0, blocking collectives: 195 us -> none  [body(): lax.psum((jnp.sum(weights, 1), jnp.sum(weights * tangent, 1), jnp.sum(ref...]
    pmax x1 -> x0, blocking collectives: 189 us -> none  [body(): top, ref_top = lax.pmax((local_top, local_ref_top), 'vocab')]
    all_gather x4 -> x0, waiting for transfers between devices: 143 us -> none  [the longest x1 77.7 us: body(): lax.all_gather(hidden, 'vocab', axis=1, tiled=True)]
    reduce_scatter x1 -> x0, waiting for transfers between devices: 114 us -> none  [body(): lax.psum_scatter(lax.dot_general(full_hidden, fisher, (((0,), (0,)), ((),...]
    pallas_call x0 -> x1, Pallas kernels: none -> 112 us  [body(): pl.pallas_call(kernel, out_shape=(jax.ShapeDtypeStruct((768, 1024), BF16)...]
    dot_general x5 -> x0, matrix products: 28.6 us -> none  [the longest x1 6.46 us: body(): lax.dot_general(full_hidden, fisher, (((0,), (0,)), ((), ())), preferred_...]
  transfers between devices with their start and end apart: 6 -> 0, of which waited for: 4 -> 0; matrix products, arithmetic and copies ran while one was open for 2% -> 0% of each run, Pallas kernels for 0% -> 0%
where the time goes in v1:
time: 128 us; the launch traced here: 125 us
  Pallas kernels  112 us (88%)
  local copies, waits for them, and re-layouts  9.53 us (7%)
  other arithmetic  3.32 us (3%)
    pallas_call x1, Pallas kernels, body(): pl.pallas_call(kernel, out_shape=(jax.ShapeDtypeStruct((768, 1024), BF16)...  112 us
    unnamed x1, local copies, waits for them, and re-layouts  2.67 us

profile of v1, /device:TPU:34, one launch (start us, length us, event | category | flops | bytes accessed | tf_op | source)
XLA Modules:
  0.0 125.5 jit_solution(11190889639366015904)
XLA Ops:
  0.6 0.7 slice.31
  1.3 1.3 %pad_add_fusion = s32[256]{0:T(256)} fusion(s32[64]{0:T(128)S(1)} %slice.31, s32[192]{0:T(256)} %param.12), kind=kLoop, calls=%fused_computation.2 | loop fusion | flops 256 | bytes 2048 | tf_op jit(solution)/shard_map/concatenate | solution.py:452
  2.6 0.7 slice.32
  3.3 1.3 %pad_add_fusion.1 = s32[256]{0:T(256)} fusion(s32[64]{0:T(128)S(1)} %slice.32, s32[192]{0:T(256)} %param.13), kind=kLoop, calls=%fused_computation.3 | loop fusion | flops 256 | bytes 2048 | tf_op jit(solution)/shard_map/concatenate | solution.py:453
  4.6 0.7 slice.38
  5.3 0.7 slice.36
  6.0 0.7 slice.39
  6.7 0.7 slice.37
  7.5 0.7 pad_maximum_fusion.s_ref
  8.2 112.0 %shard_map.102 = (bf16[768,1024]{1,0:T(8,128)(2,1)}, bf16[48,256]{1,0:T(8,128)(2,1)}, f32[2,256]{1,0:T(2,128)}) custom-call(bf16[48,384]{1,0:T(8,128)(2,1)} %pad_maximum_fusion.s_ref, bf16[768,1024]{1,0:T(8,128)(2,1)} %head_ref.1, bf16[768,1024]{1,0:T(8,128)(2,1)} %ht_ref.1, bf16[192,1024]{1,0:T(8,128)(2,1)} %ref_ref.1, s32[1,256]{1,0:T(1,128)} %bitcast.12, ...), custom_call_target="tpu_custom_call" | custom-call | tf_op jit(solution)/shard_map/pallas_call | solution.py:456
  120.2 1.3 %fusion = (f32[1,192]{1,0:T(1,128)}, f32[1,192]{1,0:T(1,128)}) fusion(f32[2,256]{1,0:T(2,128)} %get-tuple-element.9), kind=kLoop, calls=%fused_computation.4 | loop fusion | bytes 3072 | tf_op jit(solution)/shard_map/slice | solution.py:511
  121.5 1.3 %slice_bitcast_fusion = bf16[192,48]{0,1:T(8,128)(2,1)} fusion(bf16[48,256]{1,0:T(8,128)(2,1)} %get-tuple-element.8), kind=kLoop, calls=%fused_computation.1 | loop fusion | bytes 36864 | tf_op jit(solution)/shard_map/transpose | solution.py:511
  122.8 2.7 %copy.12 = bf16[768,1024]{1,0:T(8,128)(2,1)} copy(bf16[768,1024]{1,0:T(8,128)(2,1)} %get-tuple-element.16) | data formatting | bytes 3145728

commit v2 on v1

--- a/solution.py
+++ b/solution.py
@@ -40,16 +40,40 @@
     )
 
 
+class Sent:
+    def __init__(self, book, copy):
+        self.book, self.copy, self.got = book, copy, False
+
+    def start(self):
+        self.copy.start()
+        self.book.append(self)
+
+    def wait_recv(self):
+        self.copy.wait_recv()
+        self.got = True
+
+    def wait_send(self):
+        self.copy.wait_send()
+
+
 def kernel(
-    s_ref, head_ref, ht_ref, ref_ref, act_ref, val_ref,
-    hp_ref, hid_ref, tok_ref,
-    head_t, ht_t, ref_t, ybuf, hbuf, hun, tun,
+    h_ref, g_ref, head_hbm, ht_hbm, ref_hbm, act_ref, val_ref,
+    hp_hbm, hid_ref, pen_ref, alp_ref,
+    head_ref, ht_ref, ref_ref, hp_ref,
+    head_t, ht_t, ref_t, sbk, hbuf, hun, tun,
     out3, in3, out1, in1, xl, xt, rl, rt, lg, tg,
     sst, sbuf, fbuf, fun, ep,
-    e1s, e1r, e2s, e2r, zsend, zrecv, ysend, yrecv,
+    e1s, e1r, e2s, e2r, zsend, zrecv, ysend, yrecv, ysum,
+    in_sem, out_sem,
     ya_s, ya_r, za_s, za_r, xa_s, xa_r, b3_s, b3_r, b1_s, b1_r, bl_s, bl_r, bt_s, bt_r,
     c_s, c_r, d1_s, d1_r, d2_s, d2_r, d3_s, d3_r, e1_s, e1_q, e2_s, e2_q, ez_s, ez_r, ey_s, ey_r,
 ):
+    loads = [
+        pltpu.make_async_copy(src, dst, in_sem.at[i])
+        for i, (src, dst) in enumerate(((head_hbm, head_ref), (ht_hbm, ht_ref), (ref_hbm, ref_ref)))
+    ]
+    for load in loads:
+        load.start()
     v = lax.axis_index("vocab")
     t = lax.axis_index("tok")
     y, zh, x = v // 16, (v // 4) % 4, v % 4
@@ -58,6 +82,9 @@
     def at_x(d):
         return (v - x + (x + d) % 4, t)
 
+    def at_xy(dx, dy):
+        return ((y + dy) % 4 * 16 + zh * 4 + (x + dx) % 4, t)
+
     def at_y(d):
         return ((y + d) % 4 * 16 + zh * 4 + x, t)
 
@@ -67,34 +94,112 @@
     def at_z(r, d):
         return (y * 16 + (zh + d) % 4 * 4 + x, tok_of(r))
 
+    sent, loops = [], []
+
     def send(src, dst, ssem, rsem, device):
-        return pltpu.make_async_remote_copy(
-            src_ref=src, dst_ref=dst, send_sem=ssem, recv_sem=rsem,
-            device_id=device, device_id_type=MESH,
-        )
+        return Sent(
+            sent,
+            pltpu.make_async_remote_copy(
+                src_ref=src, dst_ref=dst, send_sem=ssem, recv_sem=rsem,
+                device_id=device, device_id_type=MESH,
+            ),
+        )
+
+    def raw(src, dst, ssem, rsem, device):
+        return send(src, dst, ssem, rsem, device).copy
+
+    def finish():
+        zy_finish()
+        for copy in sent:
+            copy.wait_send()
+        if loops:
+
+            @pl.loop(0, 4)
+            def _(j):
+                for copy_of in loops:
+                    copy_of(j).wait_send()
 
     barrier = pltpu.get_barrier_semaphore()
     column = [(r, d) for r in ORDER for d in range(4) if (r, d) != (0, 0)]
-    peers = [at_x(d) for d in (1, 2, 3)] + [at_y(d) for d in (1, 2, 3)] + [at_z(r, d) for r, d in column]
+    plane = [(dx, dy) for dx in range(4) for dy in range(4) if (dx, dy) != (0, 0)]
+    peers = [at_xy(dx, dy) for dx, dy in plane] + [at_z(r, d) for r, d in column]
     for peer in peers:
         pl.semaphore_signal(barrier, inc=1, device_id=peer, device_id_type=MESH)
     pl.semaphore_wait(barrier, len(peers))
 
-    y_copies = [send(s_ref, ybuf.at[y], ya_s.at[d], ya_r.at[d], at_y(d + 1)) for d in range(3)]
-    for copy in y_copies:
-        copy.start()
-    ybuf[y] = s_ref[...]
-    for copy in y_copies:
-        copy.wait_recv()
-
-    z_copies = {
-        (r, d): send(ybuf.at[tok_of(r)], hbuf.at[r, zh, x], za_s.at[r * 4 + d], za_r.at[r * 4 + d], at_z(r, d))
-        for r, d in column
-    }
-    for key in column:
-        z_copies[key].start()
-    hbuf[0, zh, x] = ybuf[t]
-
+    h, g = h_ref[...].astype(F32), g_ref[...].astype(F32)
+    sbk[:, 0:128] = h[:, 0:128].astype(BF16)
+    sbk[:, 128:256] = g[:, 0:128].astype(BF16)
+    sbk[:, 256:384] = jnp.concatenate([h[:, 128:192], g[:, 128:192]], axis=1).astype(BF16)
+    slot = (zl + y // 2) % 2 * 2 + (c + y % 2) % 2
+
+    def z_copy(d):
+        device = (y * 16 + (zh + d) % 4 * 4 + x, y)
+        return raw(sbk, hbuf.at[slot, zh, x], za_s.at[d], za_r.at[slot * 4 + d], device)
+
+    def z_wait(r, d):
+        into = hbuf.at[r, (zh + 4 - d) % 4, x]
+        raw(sbk, into, za_s.at[d], za_r.at[r * 4 + d], at_z(r, 1)).wait_recv()
+
+    for d in (1, 2, 3):
+        z_copy(d).start()
+
+    @pl.when(t != y)
+    def _():
+        z_copy(0).start()
+
+    @pl.when(t == y)
+    def _():
+        hbuf[0, zh, x] = sbk[...]
+
+    away = (y + 4 - t) % 4
+
+    def y_copy(r, k):
+        part = hbuf.at[r, :, x] if k < 2 else hbuf.at[r, (k - 2) * 2 : (k - 2) * 2 + 2, x]
+        return raw(part, part, ya_s.at[r, k], ya_r.at[r, k], at_y(3 if k % 2 else 1))
+
+    def y_stage(r):
+        @pl.when(away == 0)
+        def _():
+            for d in range(4):
+                if (r, d) != (0, 0):
+                    z_wait(r, d)
+            y_copy(r, 0).start()
+            y_copy(r, 1).start()
+
+        @pl.when(away == 1)
+        def _():
+            y_copy(r, 0).wait_recv()
+            y_copy(r, 2).start()
+
+        @pl.when(away == 3)
+        def _():
+            y_copy(r, 1).wait_recv()
+            y_copy(r, 3).start()
+
+        @pl.when(away == 2)
+        def _():
+            y_copy(r, 2).wait_recv()
+            y_copy(r, 3).wait_recv()
+
+    def zy_finish():
+        for d in (1, 2, 3):
+            z_copy(d).wait_send()
+
+        @pl.when(t != y)
+        def _():
+            z_copy(0).wait_send()
+
+        for role, kinds in ((0, (0, 1)), (1, (2,)), (3, (3,))):
+
+            @pl.when(away == role)
+            def _():
+                for r in range(4):
+                    for k in kinds:
+                        y_copy(r, k).wait_send()
+
+    for load in loads:
+        load.wait()
     for j in range(4):
         for half in range(2):
             cols = slice(half * 512 + j * 128, half * 512 + j * 128 + 128)
@@ -121,9 +226,7 @@
         )
 
     def x_start(r):
-        for d in range(4):
-            if (r, d) != (0, 0):
-                z_copies[r, d].wait_recv()
+        y_stage(r)
         for copy in x_first[r]:
             copy.start()
 
@@ -162,13 +265,13 @@
     across = (v, tok_of(2))
 
     def to_sibling(j, out, into, ssem, rsem):
-        return send(out.at[j], into.at[j], ssem.at[j], rsem.at[j], sibling)
+        return raw(out.at[j], into.at[j], ssem.at[j], rsem.at[j], sibling)
 
     def cross_l(j):
-        return send(xl.at[j], rl.at[j], bl_s.at[j], bl_r.at[j], across)
+        return raw(xl.at[j], rl.at[j], bl_s.at[j], bl_r.at[j], across)
 
     def cross_t(j):
-        return send(xt.at[j], rt.at[j], bt_s.at[j], bt_r.at[j], across)
+        return raw(xt.at[j], rt.at[j], bt_s.at[j], bt_r.at[j], across)
 
     def give(r, out, into, ssem, rsem):
         @pl.loop(0, 4)
@@ -183,12 +286,10 @@
     x_start(3)
     x_start(2)
     x_forward(3)
-    x_start(1)
     x_forward(2)
-    x_start(0)
     unpack(3)
     give(3, out3, in3, b3_s, b3_r)
-    x_forward(1)
+    loops.append(lambda j: to_sibling(j, out3, in3, b3_s, b3_r))
     unpack(2)
 
     @pl.loop(0, 4)
@@ -202,9 +303,14 @@
         cross_l(j).start()
         cross_t(j).start()
 
+    loops += [cross_l, cross_t]
+    x_start(1)
+    x_start(0)
+    x_forward(1)
     x_forward(0)
     unpack(1)
     give(1, out1, in1, b1_s, b1_r)
+    loops.append(lambda j: to_sibling(j, out1, in1, b1_s, b1_r))
     unpack(0)
 
     @pl.loop(0, 4)
@@ -241,8 +347,9 @@
     main_col = jnp.where(row < 128, row, row + 384)
     tail_row = lax.broadcasted_iota(jnp.int32, (128, 128), 0)
     tail_col = jnp.where(low128, tail_row, tail_row + 512)
-    wanted_m = act_ref[:, 0:128] - v * 1024
-    wanted_t = act_ref[:, 128:256] - v * 1024
+    wanted = act_ref[...] - v * 1024
+    wanted_m = wanted[:, 0:128]
+    wanted_t = jnp.concatenate([wanted[:, 128:192]] * 2, axis=1)
 
     def sums(j, carry):
         def part(logits, tangent, ref, top, ref_top, col, wanted, old):
@@ -265,36 +372,40 @@
     for i in range(7):
         sst[0, i : i + 1, 0:128] = rows_m[i]
         sst[0, i : i + 1, 128:256] = rows_t[i]
-    sst[:, 7:8] = jnp.zeros((3, 1, 256), F32)
-
-    c_copies = []
-    for k, place in enumerate((at_x, at_y, lambda d: at_z(0, d))):
-        now = [send(sst.at[k], sbuf.at[k, d], c_s.at[k, d], c_r.at[k, d], place(d + 1)) for d in range(3)]
-        for copy in now:
-            copy.start()
-        for copy in now:
-            copy.wait_recv()
-        merged = merge([sst[k], sbuf[k, 0], sbuf[k, 1], sbuf[k, 2]])
-        if k < 2:
-            for i in range(7):
-                sst[k + 1, i : i + 1] = merged[i]
-        c_copies += now
+    sst[:, 7:8] = jnp.zeros((2, 1, 256), F32)
+
+    now = [send(sst.at[0], sbuf.at[i], c_s.at[i], c_r.at[i], at_xy(*plane[i])) for i in range(15)]
+    for copy in now:
+        copy.start()
+    for copy in now:
+        copy.wait_recv()
+    merged = merge([sst[0]] + [sbuf[i] for i in range(15)])
+    for i in range(7):
+        sst[1, i : i + 1] = merged[i]
+    now = [send(sst.at[1], sbuf.at[i], c_s.at[i], c_r.at[i], at_z(0, i - 14)) for i in range(15, 18)]
+    for copy in now:
+        copy.start()
+    for copy in now:
+        copy.wait_recv()
+    merged = merge([sst[1]] + [sbuf[i] for i in range(15, 18)])
 
     top, total, moment, ref_top, ref_sum, cross, chosen = merged
     log_total = top + jnp.log(total)
     mean_tangent = moment / total
     valid = val_ref[...].astype(F32)
-    tok_ref[0:1] = valid * (cross / ref_sum - (ref_top + jnp.log(ref_sum)) + log_total)
-    tok_ref[1:2] = chosen - log_total
+    valid = jnp.concatenate([valid, valid[:, 128:192]], axis=1)
+    penalty = valid * (cross / ref_sum - (ref_top + jnp.log(ref_sum)) + log_total)
+    pen_ref[...] = penalty[:, 0:192]
+    alp_ref[...] = (chosen - log_total)[:, 0:192]
 
     def d_sibling(j):
-        return send(fbuf.at[0, j], fbuf.at[1, j], d1_s.at[j], d1_r.at[j], sibling)
+        return raw(fbuf.at[0, j], fbuf.at[1, j], d1_s.at[j], d1_r.at[j], sibling)
 
     def d_across(j):
-        return send(fbuf.at[0, j], fbuf.at[2, j], d2_s.at[j], d2_r.at[j], across)
+        return raw(fbuf.at[0, j], fbuf.at[2, j], d2_s.at[j], d2_r.at[j], across)
 
     def d_relay(j):
-        return send(fbuf.at[2, j], fbuf.at[3, j], d3_s.at[j], d3_r.at[j], sibling)
+        return raw(fbuf.at[2, j], fbuf.at[3, j], d3_s.at[j], d3_r.at[j], sibling)
 
     @pl.loop(0, 4)
     def _(j):
@@ -375,6 +486,7 @@
                 if (r, d) != (0, 0):
                     ez[r, d].start()
 
+    loops += [d_across, d_sibling]
     unpack_fisher(0)
     for j in range(4):
         d_sibling(j).wait_recv()
@@ -387,24 +499,37 @@
     for j in range(2, 4):
         d_across(j).wait_recv()
         d_relay(j).start()
+    loops.append(d_relay)
+    e_second(0)
     unpack_fisher(2)
     for j in range(4):
         d_relay(j).wait_recv()
     unpack_fisher(3)
     hidden_part(1)
     e_first(1)
-    e_second(0)
+
+    def product(k):
+        rows = slice(k * 256, k * 256 + 256)
+        return pltpu.make_async_copy(hp_ref.at[rows], hp_hbm.at[rows], out_sem.at[k])
+
+    def head_part(k):
+        rows = slice(k * 256, k * 256 + 256)
+
+        @pl.loop(0, 2)
+        def _(n):
+            cols = pl.ds(pl.multiple_of(n * 512, 512), 512)
+            hp_ref[rows, cols] = lax.dot_general(
+                hun[rows, :], fun[cols, :], (((1,), (1,)), ((), ())), preferred_element_type=F32
+            ).astype(BF16)
+
+        product(k).start()
+
+    e_third(0)
+    head_part(0)
     e_second(1)
-
-    @pl.loop(0, 3)
-    def _(k):
-        rows = pl.ds(pl.multiple_of(k * 256, 256), 256)
-        hp_ref[rows, :] = lax.dot_general(
-            hun[rows, :], fun[...], (((1,), (1,)), ((), ())), preferred_element_type=F32
-        ).astype(BF16)
-
-    e_third(0)
+    head_part(1)
     e_third(1)
+    head_part(2)
     for r in ORDER:
         parts = []
         for d in range(4):
@@ -414,10 +539,12 @@
             else:
                 parts.append(zsend[0, zh].astype(F32))
         whole = sum(parts)
-        slot = tok_of(r)
-        ysend[slot, :, 0:128] = whole[:, 0:128]
-        tail = whole[:, 128:256]
-        ysend[slot, :, 128:256] = swap_halves(tail) if r % 2 else tail
+        place = tok_of(r)
+        tail = swap_halves(whole[:, 128:256]) if r % 2 else whole[:, 128:256]
+        ysum[place, :, 0:128] = whole[:, 0:128]
+        ysum[place, :, 128:256] = tail
+        ysend[place, :, 0:128] = whole[:, 0:128].astype(BF16)
+        ysend[place, :, 128:256] = tail.astype(BF16)
     ey = [
         send(ysend.at[(y + d + 1) % 4], yrecv.at[d], ey_s.at[d], ey_r.at[d], at_y(d + 1)) for d in range(3)
     ]
@@ -425,48 +552,59 @@
         copy.start()
     for copy in ey:
         copy.wait_recv()
-    hid_ref[...] = (ysend[y] + yrecv[0] + yrecv[1] + yrecv[2]).astype(BF16)
-
-    for copy in y_copies + list(z_copies.values()) + c_copies + list(ez.values()) + ey:
-        copy.wait_send()
-    for copies in list(x_first.values()) + list(x_second.values()):
-        for copy in copies:
-            copy.wait_send()
-    for copy in list(e1.values()) + list(e2.values()):
-        copy.wait_send()
-
-    @pl.loop(0, 4)
-    def _(j):
-        to_sibling(j, out3, in3, b3_s, b3_r).wait_send()
-        to_sibling(j, out1, in1, b1_s, b1_r).wait_send()
-        cross_l(j).wait_send()
-        cross_t(j).wait_send()
-        d_sibling(j).wait_send()
-        d_across(j).wait_send()
-        d_relay(j).wait_send()
+    total_y = ysum[y] + sum(yrecv[d].astype(F32) for d in range(3))
+    hid_ref[...] = total_y[:, 0:192].astype(BF16)
+    finish()
+    for k in range(3):
+        product(k).wait()
+
+
+def copy_out(*refs):
+    big, in_sem, out_sem = refs[8:]
+    copies = []
+    for k in range(4):
+        rows = slice(k * 192, k * 192 + 192)
+        copies.append(
+            (
+                pltpu.make_async_copy(refs[0].at[rows], big.at[rows], in_sem.at[k]),
+                pltpu.make_async_copy(big.at[rows], refs[4].at[rows], out_sem.at[k]),
+            )
+        )
+    for load, _ in copies:
+        load.start()
+    for i in range(1, 4):
+        refs[4 + i][...] = refs[i][...]
+    for load, store in copies:
+        load.wait()
+        store.start()
+    for _, store in copies:
+        store.wait()
 
 
 def body(hidden, hidden_tangent, head, head_tangent, ref_logits, actions, valid):
-    h, g = hidden.T, hidden_tangent.T
-    stacked = jnp.concatenate([h[:, 0:128], g[:, 0:128], h[:, 128:192], g[:, 128:192]], axis=1)
-    acts = jnp.concatenate([actions, actions[128:]])[None, :]
-    flags = jnp.concatenate([valid, valid[128:]])[None, :]
     vm, dma = pltpu.VMEM, pltpu.SemaphoreType.DMA
     vmem = pl.BlockSpec(memory_space=pltpu.VMEM)
-    head_product, hid, tok = pl.pallas_call(
+    hbm = pl.BlockSpec(memory_space=pl.ANY)
+    shapes = (
+        jax.ShapeDtypeStruct((768, 1024), BF16),
+        jax.ShapeDtypeStruct((48, 192), BF16),
+        jax.ShapeDtypeStruct((1, 192), F32),
+        jax.ShapeDtypeStruct((1, 192), F32),
+    )
+    results = pl.pallas_call(
         kernel,
-        out_shape=(
-            jax.ShapeDtypeStruct((768, 1024), BF16),
-            jax.ShapeDtypeStruct((48, 256), BF16),
-            jax.ShapeDtypeStruct((2, 256), F32),
-        ),
-        in_specs=[vmem] * 6,
-        out_specs=(vmem,) * 3,
+        out_shape=shapes,
+        in_specs=[vmem, vmem, hbm, hbm, hbm, vmem, vmem],
+        out_specs=(hbm, vmem, vmem, vmem),
         scratch_shapes=[
+            vm((768, 1024), BF16),
+            vm((768, 1024), BF16),
+            vm((192, 1024), BF16),
+            vm((768, 1024), BF16),
             vm((4, 256, 768), BF16),
             vm((4, 256, 768), BF16),
             vm((4, 384, 128), F32),
-            vm((4, 48, 384), BF16),
+            vm((48, 384), BF16),
             vm((4, 4, 4, 48, 384), BF16),
             vm((768, 1024), BF16),
             vm((768, 256), BF16),
@@ -480,8 +618,8 @@
             vm((4, 384, 128), BF16),
             vm((4, 384, 128), F32),
             vm((4, 384, 128), F32),
-            vm((3, 8, 256), F32),
-            vm((3, 3, 8, 256), F32),
+            vm((2, 8, 256), F32),
+            vm((18, 8, 256), F32),
             vm((4, 4, 384, 128), BF16),
             vm((1024, 1024), BF16),
             vm((2, 4, 4, 48, 384), F32),
@@ -491,14 +629,16 @@
             vm((2, 2, 4, 48, 384), BF16),
             vm((4, 4, 48, 256), BF16),
             vm((4, 4, 48, 256), BF16),
+            vm((4, 48, 256), BF16),
+            vm((3, 48, 256), BF16),
             vm((4, 48, 256), F32),
-            vm((3, 48, 256), F32),
             dma((3,)), dma((3,)),
-            dma((16,)), dma((16,)),
+            dma((4, 4)), dma((4, 4)),
+            dma((4,)), dma((16,)),
             dma((4, 4)), dma((4, 4)),
             dma((4,)), dma((4,)), dma((4,)), dma((4,)),
             dma((4,)), dma((4,)), dma((4,)), dma((4,)),
-            dma((3, 3)), dma((3, 3)),
+            dma((18,)), dma((18,)),
             dma((4,)), dma((4,)), dma((4,)), dma((4,)), dma((4,)), dma((4,)),
             dma((2, 2)), dma((2, 2)), dma((2, 2)), dma((2, 2)),
             dma((16,)), dma((16,)),
@@ -507,8 +647,15 @@
         compiler_params=pltpu.CompilerParams(
             collective_id=0, has_side_effects=True, vmem_limit_bytes=56 * 1024 * 1024
         ),
-    )(stacked, head, head_tangent, ref_logits, acts, flags)
-    return (head_product, hid[:, 0:192].T, tok[0, 0:192], tok[1, 0:192])
+    )(hidden.T, hidden_tangent.T, head, head_tangent, ref_logits, actions[None, :], valid[None, :])
+    head_product, hid, penalty, logprob = pl.pallas_call(
+        copy_out,
+        out_shape=shapes,
+        in_specs=[hbm, vmem, vmem, vmem],
+        out_specs=(hbm, vmem, vmem, vmem),
+        scratch_shapes=[vm((768, 1024), BF16), dma((4,)), dma((4,))],
+    )(*results)
+    return (head_product, hid.T, penalty.reshape(192), logprob.reshape(192))
 
 
 def solution(mesh):

time: 128 us -> 113 us (0.88); the launches traced: 125 us -> 113 us
  local copies, waits for them, and re-layouts: 9.53 us -> 0 us
  other arithmetic: 3.32 us -> 0 us
    slice x7 -> x0, local copies, waits for them, and re-layouts: 5.52 us -> none  [the longest x1 1.32 us: body(): return (head_product, hid[:, 0:192].T, tok[0, 0:192], tok[1, 0:192])]
    concatenate x3 -> x0, other arithmetic: 3.32 us -> none  [the longest x1 1.31 us: body(): acts = jnp.concatenate([actions, actions[128:]])[None, :]]
    unnamed x1 -> x0, local copies, waits for them, and re-layouts: 2.67 us -> none
    transpose x1 -> x0, local copies, waits for them, and re-layouts: 1.35 us -> none  [body(): return (head_product, hid[:, 0:192].T, tok[0, 0:192], tok[1, 0:192])]
    pallas_call x1 -> x2, Pallas kernels: 112 us -> 112 us  [the longest x1 109 us: body(): pl.pallas_call(kernel, out_shape=shapes, in_specs=[vmem, vmem, hbm, hbm,...]
where the time goes in v2:
time: 113 us
  Pallas kernels  112 us (99%)
    pallas_call x1, Pallas kernels, body(): pl.pallas_call(kernel, out_shape=shapes, in_specs=[vmem, vmem, hbm, hbm,...  109 us
    pallas_call x1, Pallas kernels, body(): pl.pallas_call(copy_out, out_shape=shapes, in_specs=[hbm, vmem, vmem, vme...  3.56 us

profile of v2, /device:TPU:34, one launch (start us, length us, event | category | flops | bytes accessed | tf_op | source)
XLA Modules:
  0.0 113.1 jit_solution(7976800953783157753)
XLA Ops:
  0.6 108.9 %shard_map.102 = (bf16[768,1024]{1,0:T(8,128)(2,1)}, bf16[48,192]{1,0:T(8,128)(2,1)}, f32[1,192]{1,0:T(1,128)}, f32[1,192]{1,0:T(1,128)}) custom-call(bf16[48,192]{1,0:T(8,128)(2,1)} %bitcast.7, bf16[48,192]{1,0:T(8,128)(2,1)} %bitcast.8, bf16[768,1024]{1,0:T(8,128)(2,1)} %head_hbm.1, bf16[768,1024]{1,0:T(8,128)(2,1)} %ht_hbm.1, bf16[192,1024]{1,0:T(8,128)(2,1)} %ref_hbm.1, ...), custom_call_target="tpu_custom_call" | custom-call | tf_op jit(solution)/shard_map/pallas_call | solution.py:594
  109.6 3.6 %shard_map.103 = (bf16[768,1024]{1,0:T(8,128)(2,1)}, bf16[48,192]{1,0:T(8,128)(2,1)}, f32[1,192]{1,0:T(1,128)}, f32[1,192]{1,0:T(1,128)}) custom-call(bf16[768,1024]{1,0:T(8,128)(2,1)} %get-tuple-element.12.refs_0_, bf16[48,192]{1,0:T(8,128)(2,1)} %get-tuple-element.13.refs_1_, f32[1,192]{1,0:T(1,128)} %get-tuple-element.14.refs_2_, ...), custom_call_target="tpu_custom_call" | custom-call | tf_op jit(solution)/shard_map/pallas_call | solution.py:651

commit v3 on v2

--- a/solution.py
+++ b/solution.py
@@ -57,8 +57,9 @@
 
 
 def kernel(
-    h_ref, g_ref, head_hbm, ht_hbm, ref_hbm, act_ref, val_ref,
-    hp_hbm, hid_ref, pen_ref, alp_ref,
+    h_hbm, g_hbm, head_hbm, ht_hbm, ref_hbm, act_hbm, val_hbm,
+    hp_hbm, hid_hbm, pen_hbm, alp_hbm,
+    h_ref, g_ref, act_ref, val_ref, hid_ref, pen_ref, alp_ref,
     head_ref, ht_ref, ref_ref, hp_ref,
     head_t, ht_t, ref_t, sbk, hbuf, hun, tun,
     out3, in3, out1, in1, xl, xt, rl, rt, lg, tg,
@@ -70,7 +71,12 @@
 ):
     loads = [
         pltpu.make_async_copy(src, dst, in_sem.at[i])
-        for i, (src, dst) in enumerate(((head_hbm, head_ref), (ht_hbm, ht_ref), (ref_hbm, ref_ref)))
+        for i, (src, dst) in enumerate(
+            (
+                (h_hbm, h_ref), (g_hbm, g_ref), (head_hbm, head_ref), (ht_hbm, ht_ref),
+                (ref_hbm, ref_ref), (act_hbm, act_ref), (val_hbm, val_ref),
+            )
+        )
     ]
     for load in loads:
         load.start()
@@ -125,12 +131,31 @@
     peers = [at_xy(dx, dy) for dx, dy in plane] + [at_z(r, d) for r, d in column]
     for peer in peers:
         pl.semaphore_signal(barrier, inc=1, device_id=peer, device_id_type=MESH)
-    pl.semaphore_wait(barrier, len(peers))
-
+    for load in loads:
+        load.wait()
     h, g = h_ref[...].astype(F32), g_ref[...].astype(F32)
     sbk[:, 0:128] = h[:, 0:128].astype(BF16)
     sbk[:, 128:256] = g[:, 0:128].astype(BF16)
     sbk[:, 256:384] = jnp.concatenate([h[:, 128:192], g[:, 128:192]], axis=1).astype(BF16)
+
+    def turn(src, dst, j):
+        for half in range(2):
+            cols = slice(half * 512 + j * 128, half * 512 + j * 128 + 128)
+            dst[j, half * 128 : half * 128 + 128] = src[:, cols].T
+
+    def turn_ref(j):
+        a, b = slice(j * 128, j * 128 + 128), slice(512 + j * 128, 512 + j * 128 + 128)
+        ref_t[j, 0:128] = ref_ref[0:128, a].astype(F32).T
+        ref_t[j, 128:256] = ref_ref[0:128, b].astype(F32).T
+        tails = jnp.concatenate([ref_ref[128:192, a].astype(F32), ref_ref[128:192, b].astype(F32)], axis=0)
+        ref_t[j, 256:384] = tails.T
+
+    turn(head_ref, head_t, 0)
+    turn(head_ref, head_t, 1)
+    turn(head_ref, head_t, 2)
+
+    pl.semaphore_wait(barrier, len(peers))
+
     slot = (zl + y // 2) % 2 * 2 + (c + y % 2) % 2
 
     def z_copy(d):
@@ -197,18 +222,6 @@
                 for r in range(4):
                     for k in kinds:
                         y_copy(r, k).wait_send()
-
-    for load in loads:
-        load.wait()
-    for j in range(4):
-        for half in range(2):
-            cols = slice(half * 512 + j * 128, half * 512 + j * 128 + 128)
-            head_t[j, half * 128 : half * 128 + 128] = head_ref[:, cols].T
-            ht_t[j, half * 128 : half * 128 + 128] = ht_ref[:, cols].T
-            ref_t[j, half * 128 : half * 128 + 128] = ref_ref[0:128, cols].astype(F32).T
-        a, b = slice(j * 128, j * 128 + 128), slice(512 + j * 128, 512 + j * 128 + 128)
-        tails = jnp.concatenate([ref_ref[128:192, a].astype(F32), ref_ref[128:192, b].astype(F32)], axis=0)
-        ref_t[j, 256:384] = tails.T
 
     left_x, right_x = (x + 3) % 4, (x + 1) % 4
     x_first, x_second = {}, {}
@@ -283,10 +296,15 @@
             out[j, 1, 256:384] = tt
             to_sibling(j, out, into, ssem, rsem).start()
 
+    turn(head_ref, head_t, 3)
     x_start(3)
+    turn(ht_ref, ht_t, 0)
     x_start(2)
+    turn(ht_ref, ht_t, 1)
     x_forward(3)
+    turn(ht_ref, ht_t, 2)
     x_forward(2)
+    turn(ht_ref, ht_t, 3)
     unpack(3)
     give(3, out3, in3, b3_s, b3_r)
     loops.append(lambda j: to_sibling(j, out3, in3, b3_s, b3_r))
@@ -307,6 +325,8 @@
     x_start(1)
     x_start(0)
     x_forward(1)
+    for j in range(4):
+        turn_ref(j)
     x_forward(0)
     unpack(1)
     give(1, out1, in1, b1_s, b1_r)
@@ -397,6 +417,12 @@
     penalty = valid * (cross / ref_sum - (ref_top + jnp.log(ref_sum)) + log_total)
     pen_ref[...] = penalty[:, 0:192]
     alp_ref[...] = (chosen - log_total)[:, 0:192]
+    leaving = [
+        pltpu.make_async_copy(pen_ref, pen_hbm, out_sem.at[3]),
+        pltpu.make_async_copy(alp_ref, alp_hbm, out_sem.at[4]),
+    ]
+    for copy in leaving:
+        copy.start()
 
     def d_sibling(j):
         return raw(fbuf.at[0, j], fbuf.at[1, j], d1_s.at[j], d1_r.at[j], sibling)
@@ -554,36 +580,33 @@
         copy.wait_recv()
     total_y = ysum[y] + sum(yrecv[d].astype(F32) for d in range(3))
     hid_ref[...] = total_y[:, 0:192].astype(BF16)
+    leaving.append(pltpu.make_async_copy(hid_ref, hid_hbm, out_sem.at[5]))
+    leaving[2].start()
     finish()
-    for k in range(3):
-        product(k).wait()
+    for copy in leaving + [product(k) for k in range(3)]:
+        copy.wait()
 
 
 def copy_out(*refs):
-    big, in_sem, out_sem = refs[8:]
-    copies = []
+    held, in_sem, out_sem = refs[8:12], refs[12], refs[13]
+    views = []
     for k in range(4):
         rows = slice(k * 192, k * 192 + 192)
-        copies.append(
-            (
-                pltpu.make_async_copy(refs[0].at[rows], big.at[rows], in_sem.at[k]),
-                pltpu.make_async_copy(big.at[rows], refs[4].at[rows], out_sem.at[k]),
-            )
-        )
-    for load, _ in copies:
+        views.append((refs[0].at[rows], held[0].at[rows], refs[4].at[rows]))
+    views += [(refs[i], held[i], refs[4 + i]) for i in range(1, 4)]
+    loads = [pltpu.make_async_copy(a, b, in_sem.at[i]) for i, (a, b, _) in enumerate(views)]
+    stores = [pltpu.make_async_copy(b, c, out_sem.at[i]) for i, (_, b, c) in enumerate(views)]
+    for load in loads:
         load.start()
-    for i in range(1, 4):
-        refs[4 + i][...] = refs[i][...]
-    for load, store in copies:
+    for load, store in zip(loads, stores):
         load.wait()
         store.start()
-    for _, store in copies:
+    for store in stores:
         store.wait()
 
 
 def body(hidden, hidden_tangent, head, head_tangent, ref_logits, actions, valid):
     vm, dma = pltpu.VMEM, pltpu.SemaphoreType.DMA
-    vmem = pl.BlockSpec(memory_space=pltpu.VMEM)
     hbm = pl.BlockSpec(memory_space=pl.ANY)
     shapes = (
         jax.ShapeDtypeStruct((768, 1024), BF16),
@@ -594,9 +617,16 @@
     results = pl.pallas_call(
         kernel,
         out_shape=shapes,
-        in_specs=[vmem, vmem, hbm, hbm, hbm, vmem, vmem],
-        out_specs=(hbm, vmem, vmem, vmem),
+        in_specs=[hbm] * 7,
+        out_specs=(hbm,) * 4,
         scratch_shapes=[
+            vm((48, 192), BF16),
+            vm((48, 192), BF16),
+            vm((1, 192), jnp.int32),
+            vm((1, 192), jnp.int32),
+            vm((48, 192), BF16),
+            vm((1, 192), F32),
+            vm((1, 192), F32),
             vm((768, 1024), BF16),
             vm((768, 1024), BF16),
             vm((192, 1024), BF16),
@@ -632,7 +662,7 @@
             vm((4, 48, 256), BF16),
             vm((3, 48, 256), BF16),
             vm((4, 48, 256), F32),
-            dma((3,)), dma((3,)),
+            dma((7,)), dma((6,)),
             dma((4, 4)), dma((4, 4)),
             dma((4,)), dma((16,)),
             dma((4, 4)), dma((4, 4)),
@@ -651,9 +681,9 @@
     head_product, hid, penalty, logprob = pl.pallas_call(
         copy_out,
         out_shape=shapes,
-        in_specs=[hbm, vmem, vmem, vmem],
-        out_specs=(hbm, vmem, vmem, vmem),
-        scratch_shapes=[vm((768, 1024), BF16), dma((4,)), dma((4,))],
+        in_specs=[hbm] * 4,
+        out_specs=(hbm,) * 4,
+        scratch_shapes=[vm(shape.shape, shape.dtype) for shape in shapes] + [dma((7,)), dma((7,))],
     )(*results)
     return (head_product, hid.T, penalty.reshape(192), logprob.reshape(192))
 

time: 113 us -> 111 us (0.982)
  Pallas kernels: 112 us -> 110 us
    pallas_call x2, Pallas kernels: 112 us -> 110 us  [the longest x1 108 us: body(): pl.pallas_call(kernel, out_shape=shapes, in_specs=[hbm] * 7, out_specs=(h...]
where the time goes in v3:
time: 111 us
  Pallas kernels  110 us (99%)
    pallas_call x1, Pallas kernels, body(): pl.pallas_call(kernel, out_shape=shapes, in_specs=[hbm] * 7, out_specs=(h...  108 us
    pallas_call x1, Pallas kernels, body(): pl.pallas_call(copy_out, out_shape=shapes, in_specs=[hbm] * 4, out_specs=...  2.26 us

profile of v3, /device:TPU:34, one launch (start us, length us, event | category | flops | bytes accessed | tf_op | source)
XLA Modules:
  0.0 111.0 jit_solution(14564565685779915485)
XLA Ops:
  0.6 108.1 %shard_map.102 = (bf16[768,1024]{1,0:T(8,128)(2,1)}, bf16[48,192]{1,0:T(8,128)(2,1)}, f32[1,192]{1,0:T(1,128)}, f32[1,192]{1,0:T(1,128)}) custom-call(bf16[48,192]{1,0:T(8,128)(2,1)} %bitcast.7, bf16[48,192]{1,0:T(8,128)(2,1)} %bitcast.8, bf16[768,1024]{1,0:T(8,128)(2,1)} %head_hbm.1, bf16[768,1024]{1,0:T(8,128)(2,1)} %ht_hbm.1, bf16[192,1024]{1,0:T(8,128)(2,1)} %ref_hbm.1, ...), custom_call_target="tpu_custom_call" | custom-call | tf_op jit(solution)/shard_map/pallas_call | solution.py:617
  108.7 2.3 %shard_map.103 = (bf16[768,1024]{1,0:T(8,128)(2,1)}, bf16[48,192]{1,0:T(8,128)(2,1)}, f32[1,192]{1,0:T(1,128)}, f32[1,192]{1,0:T(1,128)}) custom-call(bf16[768,1024]{1,0:T(8,128)(2,1)} %get-tuple-element.12.refs_0_, bf16[48,192]{1,0:T(8,128)(2,1)} %get-tuple-element.13.refs_1_, f32[1,192]{1,0:T(1,128)} %get-tuple-element.14.refs_2_, ...), custom_call_target="tpu_custom_call" | custom-call | tf_op jit(solution)/shard_map/pallas_call | solution.py:681

commit v4 on v3

--- a/solution.py
+++ b/solution.py
@@ -82,23 +82,28 @@
         load.start()
     v = lax.axis_index("vocab")
     t = lax.axis_index("tok")
-    y, zh, x = v // 16, (v // 4) % 4, v % 4
-    zl, c = t // 2, t % 2
+    y, zh, x = lax.div(v, 16), lax.rem(lax.div(v, 4), 4), lax.rem(v, 4)
+    zl, c = lax.div(t, 2), lax.rem(t, 2)
+    xs, ys, zs = ([place] + [lax.rem(place + d, 4) for d in (1, 2, 3)] for place in (x, y, zh))
+    y_base, z_base = [place * 16 for place in ys], [place * 4 for place in zs]
+    rest_x, rest_z, rest_y = v - x, v - z_base[0], v - y_base[0]
+    toks = [z + core for z in (2 * zl, 2 - 2 * zl) for core in (c, 1 - c)]
+    x_base = [rest_x - y_base[0] + place for place in xs]
 
     def at_x(d):
-        return (v - x + (x + d) % 4, t)
+        return (rest_x + xs[d], t)
 
     def at_xy(dx, dy):
-        return ((y + dy) % 4 * 16 + zh * 4 + (x + dx) % 4, t)
+        return (y_base[dy] + x_base[dx], t)
 
     def at_y(d):
-        return ((y + d) % 4 * 16 + zh * 4 + x, t)
+        return (rest_y + y_base[d], t)
 
     def tok_of(r):
-        return (zl + r // 2) % 2 * 2 + (c + r % 2) % 2
+        return toks[r]
 
     def at_z(r, d):
-        return (y * 16 + (zh + d) % 4 * 4 + x, tok_of(r))
+        return (rest_z + z_base[d], toks[r])
 
     sent, loops = [], []
 
@@ -153,17 +158,19 @@
     turn(head_ref, head_t, 0)
     turn(head_ref, head_t, 1)
     turn(head_ref, head_t, 2)
+    turn(head_ref, head_t, 3)
+    turn(ht_ref, ht_t, 0)
 
     pl.semaphore_wait(barrier, len(peers))
 
-    slot = (zl + y // 2) % 2 * 2 + (c + y % 2) % 2
+    slot = lax.rem(zl + lax.div(y, 2), 2) * 2 + lax.rem(c + y, 2)
 
     def z_copy(d):
-        device = (y * 16 + (zh + d) % 4 * 4 + x, y)
+        device = (rest_z + z_base[d], y)
         return raw(sbk, hbuf.at[slot, zh, x], za_s.at[d], za_r.at[slot * 4 + d], device)
 
     def z_wait(r, d):
-        into = hbuf.at[r, (zh + 4 - d) % 4, x]
+        into = hbuf.at[r, zs[(4 - d) % 4], x]
         raw(sbk, into, za_s.at[d], za_r.at[r * 4 + d], at_z(r, 1)).wait_recv()
 
     for d in (1, 2, 3):
@@ -177,7 +184,7 @@
     def _():
         hbuf[0, zh, x] = sbk[...]
 
-    away = (y + 4 - t) % 4
+    away = lax.rem(y + 4 - t, 4)
 
     def y_copy(r, k):
         part = hbuf.at[r, :, x] if k < 2 else hbuf.at[r, (k - 2) * 2 : (k - 2) * 2 + 2, x]
@@ -223,7 +230,7 @@
                     for k in kinds:
                         y_copy(r, k).wait_send()
 
-    left_x, right_x = (x + 3) % 4, (x + 1) % 4
+    left_x, right_x = xs[3], xs[1]
     x_first, x_second = {}, {}
     for r in ORDER:
         own = hbuf.at[r, :, x]
@@ -296,13 +303,11 @@
             out[j, 1, 256:384] = tt
             to_sibling(j, out, into, ssem, rsem).start()
 
-    turn(head_ref, head_t, 3)
+    turn(ht_ref, ht_t, 1)
     x_start(3)
-    turn(ht_ref, ht_t, 0)
+    turn(ht_ref, ht_t, 2)
     x_start(2)
-    turn(ht_ref, ht_t, 1)
     x_forward(3)
-    turn(ht_ref, ht_t, 2)
     x_forward(2)
     turn(ht_ref, ht_t, 3)
     unpack(3)
@@ -477,7 +482,7 @@
             e2[p, side] = send(e2s.at[p, side], e2r.at[p, side], e2_s.at[p, side], e2_q.at[p, side], at_x(d))
 
     def e_first(p):
-        far = (x + 2) % 4
+        far = xs[2]
         e1s[p, 0] = ep[p, 0:2, far].astype(BF16)
         e1s[p, 1] = ep[p, 2:4, far].astype(BF16)
         e1[p, 0].start()
@@ -495,7 +500,7 @@
 
     ez = {
         (r, d): send(
-            zsend.at[r, (zh + d) % 4], zrecv.at[r, d], ez_s.at[r * 4 + d], ez_r.at[r * 4 + d], at_z(r, d)
+            zsend.at[r, zs[d]], zrecv.at[r, d], ez_s.at[r * 4 + d], ez_r.at[r * 4 + d], at_z(r, d)
         )
         for r, d in column
     }
@@ -572,7 +577,7 @@
         ysend[place, :, 0:128] = whole[:, 0:128].astype(BF16)
         ysend[place, :, 128:256] = tail.astype(BF16)
     ey = [
-        send(ysend.at[(y + d + 1) % 4], yrecv.at[d], ey_s.at[d], ey_r.at[d], at_y(d + 1)) for d in range(3)
+        send(ysend.at[ys[d + 1]], yrecv.at[d], ey_s.at[d], ey_r.at[d], at_y(d + 1)) for d in range(3)
     ]
     for copy in ey:
         copy.start()

time: 111 us -> 111 us (level)
  no operation moved by 1% of the time
where the time goes in v4:
time: 111 us
  Pallas kernels  110 us (99%)
    pallas_call x1, Pallas kernels, body(): pl.pallas_call(kernel, out_shape=shapes, in_specs=[hbm] * 7, out_specs=(h...  108 us
    pallas_call x1, Pallas kernels, body(): pl.pallas_call(copy_out, out_shape=shapes, in_specs=[hbm] * 4, out_specs=...  2.26 us

profile of v4, /device:TPU:34, one launch (start us, length us, event | category | flops | bytes accessed | tf_op | source)
XLA Modules:
  0.0 110.9 jit_solution(1886049192680560999)
XLA Ops:
  0.6 108.0 %shard_map.102 = (bf16[768,1024]{1,0:T(8,128)(2,1)}, bf16[48,192]{1,0:T(8,128)(2,1)}, f32[1,192]{1,0:T(1,128)}, f32[1,192]{1,0:T(1,128)}) custom-call(bf16[48,192]{1,0:T(8,128)(2,1)} %bitcast.7, bf16[48,192]{1,0:T(8,128)(2,1)} %bitcast.8, bf16[768,1024]{1,0:T(8,128)(2,1)} %head_hbm.1, bf16[768,1024]{1,0:T(8,128)(2,1)} %ht_hbm.1, bf16[192,1024]{1,0:T(8,128)(2,1)} %ref_hbm.1, ...), custom_call_target="tpu_custom_call" | custom-call | tf_op jit(solution)/shard_map/pallas_call | solution.py:622
  108.7 2.3 %shard_map.103 = (bf16[768,1024]{1,0:T(8,128)(2,1)}, bf16[48,192]{1,0:T(8,128)(2,1)}, f32[1,192]{1,0:T(1,128)}, f32[1,192]{1,0:T(1,128)}) custom-call(bf16[768,1024]{1,0:T(8,128)(2,1)} %get-tuple-element.12.refs_0_, bf16[48,192]{1,0:T(8,128)(2,1)} %get-tuple-element.13.refs_1_, f32[1,192]{1,0:T(1,128)} %get-tuple-element.14.refs_2_, ...), custom_call_target="tpu_custom_call" | custom-call | tf_op jit(solution)/shard_map/pallas_call | solution.py:686
